TPU v7x, 32 devices: a whole 2x2x4 slice. The times are simulated.
32 devices in a mesh: member: 4 (over x, core), grid: 8 (over z, y).
Axes of the slice: x: 2, y: 2, z: 4, core: 2. Of those that a mesh axis runs over, the one named last changes fastest.
Arguments:
- features: bfloat16 [4, 32, 512, 256], P('member', None, 'grid'), may hold values from -6 to 6
- perturbation: bfloat16 [4, 32, 512, 256], P('member', None, 'grid'), may hold values from -4 to 4
- target: bfloat16 [32, 32768], P(None, 'grid'), may hold values from -8 to 8
- head_weight: bfloat16 [256, 64], replicated, may hold values from -0.375 to 0.375
- head_bias: float32 [64], replicated, may hold values from -4 to 4
Outputs:
- hidden_grad: bfloat16 [4, 32, 512, 256], P('member', None, 'grid')
- head_grad: float32 [256, 64], P('grid')
All inputs are finite; a program needn't handle non-finite values.
Results may differ from a plain program's by a relative error of at most 0.011.
Values may be sent and summed in bfloat16 or wider, within the bound.
A program may use at most 64 MiB of HBM per device.

v0:
```python
import jax
import jax.numpy as jnp
from jax import lax
from jax.sharding import PartitionSpec as P


def smooth_sign(value):
    return value / jnp.sqrt(value * value + 0.01)


def local(features, perturbation, target, head_weight, head_bias):
    members = lax.axis_size("member")
    grid_count = lax.axis_size("grid")
    band_rows = features.shape[1]
    columns = features.shape[2]
    channels = head_weight.shape[1]
    width = columns * channels
    pair_scale = 1.0 / (members - 1.0)
    pre_act = features[0].astype(jnp.float32) + perturbation[0].astype(jnp.float32)
    activated = jax.nn.silu(pre_act).astype(jnp.bfloat16)
    pred_wide = (
        jnp.einsum("rch,hk->rck", activated, head_weight, preferred_element_type=jnp.float32)
        + head_bias
    )
    pred = pred_wide.astype(jnp.bfloat16).reshape(band_rows, width)
    own_pred = pred.astype(jnp.float32)
    shard_block = lax.all_gather(pred[None], "member", axis=0, tiled=True)

    def add_partner(partner, carry):
        other = lax.dynamic_index_in_dim(shard_block, partner, 0, keepdims=False)
        return carry + smooth_sign(own_pred - other.astype(jnp.float32))

    pair_sum = lax.fori_loop(
        0, shard_block.shape[0], add_partner, jnp.zeros((band_rows, width), jnp.float32)
    )
    own_target = target.astype(jnp.float32)
    pred_grad = (smooth_sign(own_pred - own_target) - pair_sum * pair_scale).astype(jnp.bfloat16)
    grad_cells = pred_grad.reshape(band_rows, columns, channels)
    act_grad = jnp.einsum(
        "rck,hk->rch", grad_cells, head_weight, preferred_element_type=jnp.float32
    )
    gate_val = jax.nn.sigmoid(pre_act)
    hidden_grad = (act_grad * gate_val * (1.0 + pre_act * (1.0 - gate_val))).astype(jnp.bfloat16)[
        None
    ]
    head_part = jnp.einsum("rch,rck->hk", activated, grad_cells, preferred_element_type=jnp.float32)
    head_part = head_part / (members * band_rows * columns * grid_count * 1.0)
    head_rows_sum = lax.psum_scatter(
        head_part.astype(jnp.bfloat16), "grid", scatter_dimension=0, tiled=True
    ).astype(jnp.float32)
    head_grad = lax.psum(head_rows_sum, "member")
    return (hidden_grad, head_grad)


def solution(mesh):
    return jax.shard_map(
        local,
        mesh=mesh,
        in_specs=(
            P("member", None, "grid", None),
            P("member", None, "grid", None),
            P(None, "grid"),
            P(),
            P(),
        ),
        out_specs=(P("member", None, "grid", None), P("grid", None)),
        check_vma=False,
    )
```

profile of v0, /device:TPU:0, one launch (start us, length us, event | category | flops | bytes accessed | tf_op | source)
XLA Modules:
  0.0 119.2 jit_solution(1798724206557347845)
XLA Ops:
  7.2 0.0 copy-start
  7.2 0.0 copy-start.4
  7.2 0.0 all-gather.2.cloned.1.call-start
  7.2 2.2 %fusion.3 = bf16[32,64,256]{2,1,0:T(8,128)(2,1)S(1)} fusion(bf16[1,32,64,256]{3,2,1,0:T(8,128)(2,1)} %param.8, bf16[1,32,64,256]{3,2,1,0:T(8,128)(2,1)} %param.7), kind=kLoop, calls=%fused_computation.8 | loop fusion | flops 4194304 | bytes 3145728 | tf_op jit(solution)/shard_map/convert_element_type | solution.py:20
  9.4 0.0 copy-done
  9.4 0.0 copy-done.4
  9.4 0.4 fusion.8
  9.8 1.2 broadcast_in_dim_reshape.3
  11.0 0.0 all-gather.2.cloned.1.call-update
  11.0 0.0 reduce-scatter.2.cloned.1.call-start
  11.1 0.4 reshape.18
  11.5 19.1 %all-gather.2.cloned.1.call-done = bf16[4,32,4096]{2,1,0:T(8,128)(2,1)} async-done(((bf16[1,32,4096]{2,1,0:T(8,128)(2,1)}), bf16[4,32,4096]{2,1,0:T(8,128)(2,1)}) %all-gather.2.cloned.1.call-update) | async-done | bytes 1048592 | tf_op jit(solution)/shard_map/all_gather | solution.py:27
  30.6 0.0 copy-start.3
  30.6 5.3 %while.14 = (s32[]{:T(128)}, f32[32,4096]{1,0:T(8,128)S(1)}, bf16[4,32,4096]{2,1,0:T(8,128)(2,1)}, f32[32,4096]{1,0:T(8,128)S(1)}, s32[]{:T(128)}, /*index=5*/s32[]{:T(128)}) while((s32[]{:T(128)}, f32[32,4096]{1,0:T(8,128)S(1)}, bf16[4,32,4096]{2,1,0:T(8,128)(2,1)}, f32[32,4096]{1,0:T(8,128)S(1)}, s32[]{:T(128)}, ...), condition=%wide.region_1.2_spmd.clone, body=%wide.region_0.1_spmd.clone.sunk | while | flops 917507 | bytes 1835099 | solution.py:33
  30.6 1.3 %select_add_fusion.2 = f32[32,4096]{1,0:T(8,128)S(1)} fusion(f32[32,4096]{1,0:T(8,128)S(1)} %get-tuple-element.137, f32[32,4096]{1,0:T(8,128)S(1)} %get-tuple-element.145, bf16[4,32,4096]{2,1,0:T(8,128)(2,1)} %get-tuple-element.144, s32[]{:T(128)S(6)} %copy.9, pred[]{:T(512)S(6)} %compare.3), kind=kLoop, calls=%fused_computation.1.clone.1 | loop fusion | flops 917504 | bytes 1835013 | tf_op jit(solution)/shard_map/while/body/eval_jaxpr/add | solution.py:31
  32.0 1.3 %select_add_fusion.2 = f32[32,4096]{1,0:T(8,128)S(1)} fusion(f32[32,4096]{1,0:T(8,128)S(1)} %get-tuple-element.137, f32[32,4096]{1,0:T(8,128)S(1)} %get-tuple-element.145, bf16[4,32,4096]{2,1,0:T(8,128)(2,1)} %get-tuple-element.144, s32[]{:T(128)S(6)} %copy.9, pred[]{:T(512)S(6)} %compare.3), kind=kLoop, calls=%fused_computation.1.clone.1 | loop fusion | flops 917504 | bytes 1835013 | tf_op jit(solution)/shard_map/while/body/eval_jaxpr/add | solution.py:31
  33.3 1.3 %select_add_fusion.2 = f32[32,4096]{1,0:T(8,128)S(1)} fusion(f32[32,4096]{1,0:T(8,128)S(1)} %get-tuple-element.137, f32[32,4096]{1,0:T(8,128)S(1)} %get-tuple-element.145, bf16[4,32,4096]{2,1,0:T(8,128)(2,1)} %get-tuple-element.144, s32[]{:T(128)S(6)} %copy.9, pred[]{:T(512)S(6)} %compare.3), kind=kLoop, calls=%fused_computation.1.clone.1 | loop fusion | flops 917504 | bytes 1835013 | tf_op jit(solution)/shard_map/while/body/eval_jaxpr/add | solution.py:31
  34.6 1.3 %select_add_fusion.2 = f32[32,4096]{1,0:T(8,128)S(1)} fusion(f32[32,4096]{1,0:T(8,128)S(1)} %get-tuple-element.137, f32[32,4096]{1,0:T(8,128)S(1)} %get-tuple-element.145, bf16[4,32,4096]{2,1,0:T(8,128)(2,1)} %get-tuple-element.144, s32[]{:T(128)S(6)} %copy.9, pred[]{:T(512)S(6)} %compare.3), kind=kLoop, calls=%fused_computation.1.clone.1 | loop fusion | flops 917504 | bytes 1835013 | tf_op jit(solution)/shard_map/while/body/eval_jaxpr/add | solution.py:31
  35.9 0.0 copy-done.3
  36.0 0.2 subtract_convert_fusion
  36.1 0.0 copy-start.2
  36.1 1.3 %reshape.16 = bf16[32,64,64]{2,1,0:T(8,128)(2,1)} reshape(bf16[32,4096]{1,0:T(8,128)(2,1)S(1)} %subtract_convert_fusion) | data formatting | bytes 524288 | tf_op jit(solution)/shard_map/reshape | solution.py:38
  37.5 0.0 copy-start.1
  37.5 2.2 %fusion.10 = bf16[256,64]{1,0:T(8,128)(2,1)} fusion(bf16[32,64,256]{2,1,0:T(8,128)(2,1)S(1)} %fusion.3, bf16[32,64,64]{2,1,0:T(8,128)(2,1)} %reshape.16), kind=kOutput, calls=%fused_computation.18 | convolution fusion | flops 67141632 | bytes 1343488 | tf_op jit(solution)/shard_map/rch,rck->hk/dot_general | solution.py:46
  39.7 0.0 reduce-scatter.2.cloned.1.call-update
  39.7 0.0 copy-done.2
  39.7 0.0 copy-done.1
  39.8 2.9 %fusion.7 = bf16[1,32,64,256]{3,2,1,0:T(8,128)(2,1)} fusion(bf16[1,32,64,256]{3,2,1,0:T(8,128)(2,1)S(1)} %copy-done.1, bf16[1,32,64,256]{3,2,1,0:T(8,128)(2,1)S(1)} %copy-done.2, bf16[32,64,64]{2,1,0:T(8,128)(2,1)} %reshape.16, bf16[256,64]{0,1:T(8,128)(2,1)S(1)} %copy-done), kind=kOutput, calls=%fused_computation.13 | convolution fusion | flops 73400320 | bytes 3440640 | tf_op jit(solution)/shard_map/rck,hk->rch/dot_general | solution.py:39
  42.7 58.4 %reduce-scatter.2.cloned.1.call-done = bf16[32,64]{1,0:T(8,128)(2,1)} async-done(((bf16[256,64]{1,0:T(8,128)(2,1)}), bf16[32,64]{1,0:T(8,128)(2,1)}) %reduce-scatter.2.cloned.1.call-update) | async-done | bytes 4112 | tf_op jit(solution)/shard_map/reduce_scatter | solution.py:48
  101.1 11.2 %psum.7 = f32[32,64]{1,0:T(8,128)} all-reduce(bf16[32,64]{1,0:T(8,128)(2,1)} %reduce-scatter.2.cloned.1.call-done), channel_id=1, replica_groups=mesh['member'=4,'grid'=8] {'member'}, use_global_device_ids=true, to_apply=%region_3.4 | all-reduce | flops 2048 | bytes 12288 | tf_op jit(solution)/shard_map/psum | solution.py:51
  (1 shorter events, 0.0 us)
Async XLA Ops:
  7.2 2.2 %copy-start = (bf16[256,64]{0,1:T(8,128)(2,1)S(1)}, bf16[256,64]{0,1:T(8,128)(2,1)}, u32[]{:S(2)}) copy-start(bf16[256,64]{0,1:T(8,128)(2,1)} %param.10) | copy-start | bytes 98308
  7.2 2.2 %copy-start.4 = (f32[64]{0:T(128)S(1)}, f32[64]{0:T(128)}, u32[]{:S(2)}) copy-start(f32[64]{0:T(128)} %param.11) | copy-start | bytes 772
  7.2 23.4 %all-gather.2.cloned.1.call-start = ((), (), s32[]{:S(2)}) async-start(), calls=%async_computation.1 | async-start | bytes 1310720 | tf_op jit(solution)/shard_map/all_gather | solution.py:27
  11.0 90.1 %reduce-scatter.2.cloned.1.call-start = ((), (), s32[]{:S(2)}) async-start(), calls=%async_computation.2 | async-start | bytes 73728 | tf_op jit(solution)/shard_map/reduce_scatter | solution.py:48
  30.6 5.3 %copy-start.3 = (bf16[32,4096]{1,0:T(8,128)(2,1)S(1)}, bf16[32,4096]{1,0:T(8,128)(2,1)}, u32[]{:S(2)}) copy-start(bf16[32,4096]{1,0:T(8,128)(2,1)} %param.9) | copy-start | bytes 786436
  36.1 3.6 %copy-start.2 = (bf16[1,32,64,256]{3,2,1,0:T(8,128)(2,1)S(1)}, bf16[1,32,64,256]{3,2,1,0:T(8,128)(2,1)}, u32[]{:S(2)}) copy-start(bf16[1,32,64,256]{3,2,1,0:T(8,128)(2,1)} %param.7) | copy-start | bytes 3145732
  37.5 2.3 %copy-start.1 = (bf16[1,32,64,256]{3,2,1,0:T(8,128)(2,1)S(1)}, bf16[1,32,64,256]{3,2,1,0:T(8,128)(2,1)}, u32[]{:S(2)}) copy-start(bf16[1,32,64,256]{3,2,1,0:T(8,128)(2,1)} %param.8) | copy-start | bytes 3145732
Sparse Core Ops, SparseCore 0:
  11.2 19.4 all-gather.1
  39.9 61.2 reduce-scatter.1
where the time goes:
time: 120 us; the launch traced here: 119 us
  waiting for transfers between devices  77.6 us (65%)
  between operations  14.1 us (12%)
  blocking collectives  11.2 us (9%)
  other arithmetic  7.56 us (6%)
  matrix products  5.59 us (5%)
  local copies, waits for them, and re-layouts  2.96 us (2%)
    reduce_scatter x1, waiting for transfers between devices, local(): lax.psum_scatter(head_part.astype(jnp.bfloat16), 'grid', scatter_dimensio...  58.4 us
    all_gather x1, waiting for transfers between devices, local(): shard_block = lax.all_gather(pred[None], 'member', axis=0, tiled=True)  19.1 us
    psum x1, blocking collectives, local(): head_grad = lax.psum(head_rows_sum, 'member')  11.2 us
    add x4, other arithmetic, add_partner(): return carry + smooth_sign(own_pred - other.astype(jnp.float32))  5.25 us
    dot_general x1, matrix products, local(): jnp.einsum('rck,hk->rch', grad_cells, head_weight, preferred_element_type...  2.94 us
  transfers between devices with their start and end apart: 2, of which 2 were waited for; matrix products, arithmetic and copies ran while one was open for 3% of the time, Pallas kernels for 0%

commit v1 on v0

v1 whole, which is shorter than its diff:
```python
import functools

import jax
import jax.numpy as jnp
from jax import lax
from jax.experimental import pallas as pl
from jax.experimental.pallas import tpu as pltpu
from jax.sharding import PartitionSpec as P

F32 = jnp.float32
BF16 = jnp.bfloat16
LANES = 128
CHUNKS = 4
TAIL = 2


def smooth_sign(value):
    return value * lax.rsqrt(value * value + 0.01)


def kernel(
    members,
    grid_count,
    features,
    perturbation,
    target,
    weight_t,
    bias,
    hidden_grad,
    head_grad,
    feat_buf,
    pert_buf,
    target_buf,
    target_cells,
    weight_pair,
    act_buf,
    gate_buf,
    preds,
    hidden_buf,
    head_acc,
    grid_send,
    grid_recv,
    member_sum,
    in_sem,
    target_sem,
    out_sem,
    pred_send_sem,
    pred_recv_sem,
    grid_send_sem,
    grid_recv_sem,
    member_send_sem,
    member_recv_sem,
):
    _, band_rows, columns, hidden = features.shape
    channels = weight_t.shape[0]
    half = columns // 2
    rows = band_rows // CHUNKS
    cells = rows * half
    chips = members // 2
    member = lax.axis_index("member")
    grid = lax.axis_index("grid")
    core = lax.rem(member, 2)
    chip = member // 2
    sibling = chip * 2 + 1 - core

    loads = []
    for k in range(CHUNKS):
        span = pl.ds(k * rows, rows)
        pair = []
        for which, (source, buffer) in enumerate(((features, feat_buf), (perturbation, pert_buf))):
            copy = pltpu.make_async_copy(source.at[0, span], buffer.at[k], in_sem.at[which, k])
            copy.start()
            pair.append(copy)
        loads.append(pair)
    target_load = pltpu.make_async_copy(target, target_buf, target_sem)
    target_load.start()

    barrier = pltpu.get_barrier_semaphore()
    for offset in range(1, members):
        pl.semaphore_signal(
            barrier,
            inc=1,
            device_id={"member": lax.rem(member + offset, members)},
            device_id_type=pl.DeviceIdType.MESH,
        )
    for offset in range(1, grid_count):
        pl.semaphore_signal(
            barrier,
            inc=1,
            device_id={"grid": lax.rem(grid + offset, grid_count)},
            device_id_type=pl.DeviceIdType.MESH,
        )

    zero = jnp.zeros((channels, hidden), BF16)
    weight_pair[:channels, :hidden] = weight_t[...]
    weight_pair[:channels, hidden:] = zero
    weight_pair[channels:, :hidden] = zero
    weight_pair[channels:, hidden:] = weight_t[...]
    bias_pair = jnp.concatenate([bias[...], bias[...]], axis=1)

    def member_copy(source, slot, k, device):
        return pltpu.make_async_remote_copy(
            src_ref=source,
            dst_ref=preds.at[slot[0], slot[1], k],
            send_sem=pred_send_sem.at[slot[0], slot[1], k],
            recv_sem=pred_recv_sem.at[slot[0], slot[1], k],
            device_id={"member": device},
            device_id_type=pl.DeviceIdType.MESH,
        )

    def forward(k):
        for copy in loads[k]:
            copy.wait()
        for side in range(2):
            cols = pl.ds(side * half, half)
            lanes = pl.ds(side * hidden, hidden)
            pre_act = feat_buf[k, :, cols, :].astype(F32) + pert_buf[k, :, cols, :].astype(F32)
            pre_act = pre_act.reshape(cells, hidden)
            gate = 0.5 + 0.5 * jnp.tanh(0.5 * pre_act)
            activated = pre_act * gate
            act_buf[k, :, lanes] = activated.astype(BF16)
            gate_buf[k, :, lanes] = gate + activated * (1.0 - gate)
        pred = lax.dot_general(
            act_buf[k], weight_pair[...], (((1,), (1,)), ((), ())), preferred_element_type=F32
        )
        preds[0, 0, k] = (pred + bias_pair).astype(BF16)

    own_copies = []
    sib_copies = []
    for k in range(CHUNKS):
        forward(k)
        if k == 0:
            pl.semaphore_wait(barrier, members + grid_count - 2)
        across = []
        for d in range(1, chips):
            to_chip = lax.rem(chip + chips - d, chips)
            copy = member_copy(preds.at[0, 0, k], (d, 0), k, to_chip * 2 + core)
            copy.start()
            across.append(copy)
        own_copies.append(across)
        copy = member_copy(preds.at[0, 0, k], (0, 1), k, sibling)
        copy.start()
        sib_copies.append(copy)

    target_load.wait()
    low = lax.broadcasted_iota(jnp.int32, (band_rows, LANES), 1) < channels
    for i in range(half // 2):
        first = target_buf[:, pl.ds(i * LANES, LANES)].astype(F32)
        second = target_buf[:, pl.ds((half // 2 + i) * LANES, LANES)].astype(F32)
        even = jnp.where(low, first, pltpu.roll(second, channels, 1))
        odd = jnp.where(low, pltpu.roll(first, channels, 1), second)
        target_cells[pl.ds(2 * i, band_rows, stride=half), :] = even
        target_cells[pl.ds(2 * i + 1, band_rows, stride=half), :] = odd

    def backward_scores(k):
        own = preds[0, 0, k].astype(F32)
        sib_copies[k].wait_recv()
        total = smooth_sign(own - preds[0, 1, k].astype(F32))
        for d in range(1, chips):
            total += smooth_sign(own - preds[d, 0, k].astype(F32))
        score = smooth_sign(own - target_cells[pl.ds(k * cells, cells), :])
        for d in range(1, chips):
            passed_on[k][d - 1].wait_recv()
            total += smooth_sign(own - preds[d, 1, k].astype(F32))
        pred_grad = score - total * (1.0 / (members - 1.0))
        turned = pred_grad.T.astype(BF16)
        part = jnp.dot(turned, act_buf[k], preferred_element_type=F32)
        part = part[:channels, :hidden] + part[channels:, hidden:]
        if k == 0:
            head_acc[...] = part
        else:
            head_acc[...] += part
        return pred_grad.astype(BF16)

    stores = []

    def backward_hidden(k, pred_grad):
        act_grad = jnp.dot(pred_grad, weight_pair[...], preferred_element_type=F32)
        grad = (act_grad * gate_buf[k]).astype(BF16)
        for side in range(2):
            hidden_buf[k, :, pl.ds(side * half, half), :] = grad[
                :, side * hidden : (side + 1) * hidden
            ].reshape(rows, half, hidden)
        copy = pltpu.make_async_copy(
            hidden_buf.at[k], hidden_grad.at[0, pl.ds(k * rows, rows)], out_sem.at[k]
        )
        copy.start()
        stores.append(copy)

    passed_on = []
    grads = []

    def receive(k):
        passed = []
        for d in range(1, chips):
            own_copies[k][d - 1].wait_recv()
            copy = member_copy(preds.at[d, 0, k], (d, 1), k, sibling)
            copy.start()
            passed.append(copy)
        passed_on.append(passed)

    receive(0)
    for k in range(CHUNKS):
        if k + 1 < CHUNKS:
            receive(k + 1)
        grads.append(backward_scores(k))
        if k < CHUNKS - TAIL:
            backward_hidden(k, grads[k])

    packed = grid_send.shape[1]
    scaled = head_acc[...] * (1.0 / (members * band_rows * columns * grid_count))
    blocks = jnp.concatenate([scaled, scaled], axis=0).T.reshape(grid_count, 2 * packed, LANES)
    lane = lax.broadcasted_iota(jnp.int32, (grid_count, packed, LANES), 2)
    grid_send[...] = jnp.where(
        lane < channels, blocks[:, :packed], blocks[:, packed:]
    ).astype(grid_send.dtype)
    grid_copies = []
    for offset in range(1, grid_count):
        peer = lax.rem(grid + offset, grid_count)
        copy = pltpu.make_async_remote_copy(
            src_ref=grid_send.at[peer],
            dst_ref=grid_recv.at[offset - 1],
            send_sem=grid_send_sem.at[offset - 1],
            recv_sem=grid_recv_sem.at[offset - 1],
            device_id={"grid": peer},
            device_id_type=pl.DeviceIdType.MESH,
        )
        copy.start()
        grid_copies.append(copy)
    for k in range(CHUNKS - TAIL, CHUNKS):
        backward_hidden(k, grads[k])

    total = grid_send[grid].astype(F32)
    for offset in range(1, grid_count):
        grid_copies[offset - 1].wait_recv()
        total += grid_recv[offset - 1].astype(F32)
    member_sum[member] = total

    def sum_copy(slot, offset):
        return pltpu.make_async_remote_copy(
            src_ref=member_sum.at[slot],
            dst_ref=member_sum.at[slot],
            send_sem=member_send_sem.at[offset - 1],
            recv_sem=member_recv_sem.at[offset - 1],
            device_id={"member": lax.rem(member + offset, members)},
            device_id_type=pl.DeviceIdType.MESH,
        )

    sum_copies = []
    for offset in range(1, members):
        copy = sum_copy(member, offset)
        copy.start()
        sum_copies.append(copy)

    for k in range(CHUNKS):
        sib_copies[k].wait_send()
        for copy in own_copies[k]:
            copy.wait_send()
        for copy in passed_on[k]:
            copy.wait_send()
    for copy in grid_copies:
        copy.wait_send()
    for copy in stores:
        copy.wait()
    for offset in range(1, members):
        sum_copy(lax.rem(member + members - offset, members), offset).wait_recv()
    head = member_sum[0]
    for other in range(1, members):
        head += member_sum[other]
    head_grad[...] = jnp.concatenate([head[:, :channels], head[:, channels:]], axis=0)
    for copy in sum_copies:
        copy.wait_send()


def local(features, perturbation, target, head_weight, head_bias):
    members = lax.axis_size("member")
    grid_count = lax.axis_size("grid")
    _, band_rows, columns, hidden = features.shape
    channels = head_weight.shape[1]
    half = columns // 2
    rows = band_rows // CHUNKS
    cells = rows * half
    chips = members // 2
    head_rows = hidden // grid_count
    packed = head_rows // 2
    sum_dtype = BF16 if packed % 16 == 0 else F32
    dma = pltpu.SemaphoreType.DMA
    vmem = pl.BlockSpec(memory_space=pltpu.VMEM)
    hbm = pl.BlockSpec(memory_space=pl.ANY)
    return pl.pallas_call(
        functools.partial(kernel, members, grid_count),
        out_shape=(
            jax.ShapeDtypeStruct(features.shape, BF16),
            jax.ShapeDtypeStruct((head_rows, channels), F32),
        ),
        in_specs=[hbm, hbm, hbm, vmem, vmem],
        out_specs=(hbm, vmem),
        scratch_shapes=[
            pltpu.VMEM((CHUNKS, rows, columns, hidden), BF16),
            pltpu.VMEM((CHUNKS, rows, columns, hidden), BF16),
            pltpu.VMEM(target.shape, BF16),
            pltpu.VMEM((band_rows * half, LANES), F32),
            pltpu.VMEM((2 * channels, 2 * hidden), BF16),
            pltpu.VMEM((CHUNKS, cells, 2 * hidden), BF16),
            pltpu.VMEM((CHUNKS, cells, 2 * hidden), F32),
            pltpu.VMEM((chips, 2, CHUNKS, cells, LANES), BF16),
            pltpu.VMEM((CHUNKS, rows, columns, hidden), BF16),
            pltpu.VMEM((channels, hidden), F32),
            pltpu.VMEM((grid_count, packed, LANES), sum_dtype),
            pltpu.VMEM((grid_count - 1, packed, LANES), sum_dtype),
            pltpu.VMEM((members, packed, LANES), F32),
            dma((2, CHUNKS)),
            dma,
            dma((CHUNKS,)),
            dma((chips, 2, CHUNKS)),
            dma((chips, 2, CHUNKS)),
            dma((grid_count - 1,)),
            dma((grid_count - 1,)),
            dma((members - 1,)),
            dma((members - 1,)),
        ],
        compiler_params=pltpu.CompilerParams(
            collective_id=0, has_side_effects=True, vmem_limit_bytes=48 * 1024 * 1024
        ),
        cost_estimate=pl.CostEstimate(
            flops=6 * band_rows * columns * hidden * channels,
            bytes_accessed=7 * band_rows * columns * hidden,
            transcendentals=2 * band_rows * columns * hidden,
        ),
    )(features, perturbation, target, head_weight.T, head_bias[None])


def solution(mesh):
    return jax.shard_map(
        local,
        mesh=mesh,
        in_specs=(
            P("member", None, "grid", None),
            P("member", None, "grid", None),
            P(None, "grid"),
            P(),
            P(),
        ),
        out_specs=(P("member", None, "grid", None), P("grid", None)),
        check_vma=False,
    )
```

time: 120 us -> 28.4 us (0.24)
  waiting for transfers between devices: 77.6 us -> 0 us
  Pallas kernels: 0 us -> 21 us
  between operations: 14.1 us -> 0.65 us
  blocking collectives: 11.2 us -> 0 us
  other arithmetic: 7.56 us -> 0 us
  matrix products: 5.59 us -> 0 us
  local copies, waits for them, and re-layouts: 2.96 us -> 6.38 us
    reduce_scatter x1 -> x0, waiting for transfers between devices: 58.4 us -> none  [local(): lax.psum_scatter(head_part.astype(jnp.bfloat16), 'grid', scatter_dimensio...]
    pallas_call x0 -> x1, Pallas kernels: none -> 21 us  [local(): pl.pallas_call(functools.partial(kernel, members, grid_count), out_shape=...]
    all_gather x1 -> x0, waiting for transfers between devices: 19.1 us -> none  [local(): shard_block = lax.all_gather(pred[None], 'member', axis=0, tiled=True)]
    psum x1 -> x0, blocking collectives: 11.2 us -> none  [local(): head_grad = lax.psum(head_rows_sum, 'member')]
    unnamed x10 -> x12, local copies, waits for them, and re-layouts: 0.03 us -> 6.38 us
    dot_general x3 -> x0, matrix products: 5.59 us -> none  [the longest x1 2.94 us: local(): jnp.einsum('rck,hk->rch', grad_cells, head_weight, preferred_element_type...]
    add x4 -> x0, other arithmetic: 5.25 us -> none  [add_partner(): return carry + smooth_sign(own_pred - other.astype(jnp.float32))]
    convert_element_type x2 -> x0, other arithmetic: 2.32 us -> none  [the longest x1 2.16 us: local(): activated = jax.nn.silu(pre_act).astype(jnp.bfloat16)]
  transfers between devices with their start and end apart: 2 -> 0, of which waited for: 2 -> 0; matrix products, arithmetic and copies ran while one was open for 3% -> 0% of each run, Pallas kernels for 0% -> 0%
where the time goes in v1:
time: 28.4 us; the launch traced here: 28.1 us
  Pallas kernels  21 us (74%)
  local copies, waits for them, and re-layouts  6.38 us (22%)
  between operations  0.65 us (2%)
    pallas_call x1, Pallas kernels, local(): pl.pallas_call(functools.partial(kernel, members, grid_count), out_shape=...  21 us
    unnamed x12, local copies, waits for them, and re-layouts  6.38 us

profile of v1, /device:TPU:0, one launch (start us, length us, event | category | flops | bytes accessed | tf_op | source)
XLA Modules:
  0.0 28.1 jit_solution(6011886099159362173)
XLA Ops:
  0.6 0.0 copy-start.4
  0.6 0.6 %copy-done.4 = f32[64]{0:T(128)S(1)} copy-done((f32[64]{0:T(128)S(1)}, f32[64]{0:T(128)}, u32[]{:S(2)}) %copy-start.4) | copy-done | bytes 280
  1.3 0.0 copy-start
  1.3 1.2 %copy-done = bf16[1,32,64,256]{3,2,1,0:T(8,128)(2,1)S(1)} copy-done((bf16[1,32,64,256]{3,2,1,0:T(8,128)(2,1)S(1)}, bf16[1,32,64,256]{3,2,1,0:T(8,128)(2,1)}, u32[]{:S(2)}) %copy-start) | copy-done | bytes 1048600
  2.5 0.0 copy-start.1
  2.5 1.2 %copy-done.1 = bf16[1,32,64,256]{3,2,1,0:T(8,128)(2,1)S(1)} copy-done((bf16[1,32,64,256]{3,2,1,0:T(8,128)(2,1)S(1)}, bf16[1,32,64,256]{3,2,1,0:T(8,128)(2,1)}, u32[]{:S(2)}) %copy-start.1) | copy-done | bytes 1048600
  3.7 0.0 copy-start.2
  3.7 0.9 %copy-done.2 = bf16[32,4096]{1,0:T(8,128)(2,1)S(1)} copy-done((bf16[32,4096]{1,0:T(8,128)(2,1)S(1)}, bf16[32,4096]{1,0:T(8,128)(2,1)}, u32[]{:S(2)}) %copy-start.2) | copy-done | bytes 262168
  4.7 0.0 copy-start.3
  4.7 0.8 %copy-done.3 = bf16[256,64]{0,1:T(8,128)(2,1)S(1)} copy-done((bf16[256,64]{0,1:T(8,128)(2,1)S(1)}, bf16[256,64]{0,1:T(8,128)(2,1)}, u32[]{:S(2)}) %copy-start.3) | copy-done | bytes 32792
  5.4 21.0 %shard_map.68 = (bf16[1,32,64,256]{3,2,1,0:T(8,128)(2,1)S(1)}, f32[32,64]{1,0:T(8,128)S(1)}) custom-call(bf16[1,32,64,256]{3,2,1,0:T(8,128)(2,1)S(1)} %copy-done, bf16[1,32,64,256]{3,2,1,0:T(8,128)(2,1)S(1)} %copy-done.1, bf16[32,4096]{1,0:T(8,128)(2,1)S(1)} %copy-done.2, bf16[64,256]{1,0:T(8,128)(2,1)S(1)} %bitcast.2, f32[1,64]{1,0:T(1,128)S(1)} %bitcast.3), custom_call_target="tpu_custom_call" | custom-call | flops 201326592 | bytes 3670016 | tf_op jit(solution)/shard_map/pallas_call | solution.py:290
  26.5 1.0 %copy.9 = bf16[1,32,64,256]{3,2,1,0:T(8,128)(2,1)} copy(bf16[1,32,64,256]{3,2,1,0:T(8,128)(2,1)S(1)} %get-tuple-element.4) | data formatting | bytes 2097152
  27.4 0.6 %copy.10 = f32[32,64]{1,0:T(8,128)} copy(f32[32,64]{1,0:T(8,128)S(1)} %get-tuple-element.5) | data formatting | bytes 16384
Async XLA Ops:
  0.6 0.7 %copy-start.4 = (f32[64]{0:T(128)S(1)}, f32[64]{0:T(128)}, u32[]{:S(2)}) copy-start(f32[64]{0:T(128)} %param.9) | copy-start | bytes 772
  1.3 1.2 %copy-start = (bf16[1,32,64,256]{3,2,1,0:T(8,128)(2,1)S(1)}, bf16[1,32,64,256]{3,2,1,0:T(8,128)(2,1)}, u32[]{:S(2)}) copy-start(bf16[1,32,64,256]{3,2,1,0:T(8,128)(2,1)} %features.1) | copy-start | bytes 3145732
  2.5 1.2 %copy-start.1 = (bf16[1,32,64,256]{3,2,1,0:T(8,128)(2,1)S(1)}, bf16[1,32,64,256]{3,2,1,0:T(8,128)(2,1)}, u32[]{:S(2)}) copy-start(bf16[1,32,64,256]{3,2,1,0:T(8,128)(2,1)} %perturbation.1) | copy-start | bytes 3145732
  3.7 0.9 %copy-start.2 = (bf16[32,4096]{1,0:T(8,128)(2,1)S(1)}, bf16[32,4096]{1,0:T(8,128)(2,1)}, u32[]{:S(2)}) copy-start(bf16[32,4096]{1,0:T(8,128)(2,1)} %target.1) | copy-start | bytes 786436
  4.7 0.8 %copy-start.3 = (bf16[256,64]{0,1:T(8,128)(2,1)S(1)}, bf16[256,64]{0,1:T(8,128)(2,1)}, u32[]{:S(2)}) copy-start(bf16[256,64]{0,1:T(8,128)(2,1)} %param.8) | copy-start | bytes 98308

commit v2 on v1

v2 whole, which is shorter than its diff:
```python
import functools

import jax
import jax.numpy as jnp
from jax import lax
from jax.experimental import pallas as pl
from jax.experimental.pallas import tpu as pltpu
from jax.sharding import PartitionSpec as P

F32 = jnp.float32
BF16 = jnp.bfloat16
LANES = 128
CHUNKS = 8
TAIL = 2
DIRECT = 1


def smooth_sign(value):
    return value * lax.rsqrt(value * value + 0.01)


def kernel(
    members,
    grid_count,
    features,
    perturbation,
    target,
    weight_hbm,
    bias_hbm,
    hidden_grad,
    head_grad,
    weight_t,
    bias,
    feat_buf,
    pert_buf,
    target_buf,
    target_cells,
    weight_pair,
    act_buf,
    sibling_act,
    gate_buf,
    preds,
    head_acc,
    sum_send,
    sum_recv,
    in_sem,
    small_sem,
    target_sem,
    pred_send_sem,
    pred_recv_sem,
    act_send_sem,
    act_recv_sem,
    sum_send_sem,
    sum_recv_sem,
):
    _, band_rows, columns, hidden = features.shape
    channels = weight_hbm.shape[0]
    half = columns // 2
    half_hidden = hidden // 2
    half_grid = grid_count // 2
    rows = band_rows // CHUNKS
    cells = rows * half
    chips = members // 2
    member = lax.axis_index("member")
    grid = lax.axis_index("grid")
    core = lax.rem(member, 2)
    chip = member // 2
    sibling = chip * 2 + 1 - core
    owner_core = grid // half_grid
    own_sum = core == owner_core
    mesh_ids = pl.DeviceIdType.MESH

    small_loads = []
    for which, (source, buffer) in enumerate(((weight_hbm, weight_t), (bias_hbm, bias))):
        copy = pltpu.make_async_copy(source, buffer, small_sem.at[which])
        copy.start()
        small_loads.append(copy)
    loads = []
    for k in range(CHUNKS):
        span = pl.ds(k * rows, rows)
        pair = []
        for which, (source, buffer) in enumerate(((features, feat_buf), (perturbation, pert_buf))):
            copy = pltpu.make_async_copy(source.at[0, span], buffer.at[k], in_sem.at[which, k])
            copy.start()
            pair.append(copy)
        loads.append(pair)
    target_load = pltpu.make_async_copy(target, target_buf, target_sem)
    target_load.start()

    barrier = pltpu.get_barrier_semaphore()

    def greet(device):
        pl.semaphore_signal(barrier, inc=1, device_id=device, device_id_type=mesh_ids)

    for offset in range(1, members):
        greet({"member": lax.rem(member + offset, members)})
    for q in range(chips):
        for i in range(grid_count):
            device = {
                "member": lax.rem(chip + q, chips) * 2 + owner_core,
                "grid": lax.rem(grid + i, grid_count),
            }
            if q == 0 and i == 0:
                pl.when(jnp.logical_not(own_sum))(functools.partial(greet, device))
            else:
                greet(device)

    for copy in small_loads:
        copy.wait()
    zero = jnp.zeros((channels, half_hidden), BF16)
    for part in range(2):
        lanes = pl.ds(part * half_hidden, half_hidden)
        weight_pair[part, :channels, :half_hidden] = weight_t[:, lanes]
        weight_pair[part, :channels, half_hidden:] = zero
        weight_pair[part, channels:, :half_hidden] = zero
        weight_pair[part, channels:, half_hidden:] = weight_t[:, lanes]
    bias_pair = jnp.concatenate([bias[...], bias[...]], axis=1)

    def member_copy(source, slot, k, device):
        return pltpu.make_async_remote_copy(
            src_ref=source,
            dst_ref=preds.at[slot[0], slot[1], k],
            send_sem=pred_send_sem.at[slot[0], slot[1], k],
            recv_sem=pred_recv_sem.at[slot[0], slot[1], k],
            device_id={"member": device},
            device_id_type=mesh_ids,
        )

    def forward(k):
        for copy in loads[k]:
            copy.wait()
        for side in range(2):
            cols = pl.ds(side * half, half)
            lanes = pl.ds(side * half_hidden, half_hidden)
            pre_act = feat_buf[k, :, cols, :].astype(F32) + pert_buf[k, :, cols, :].astype(F32)
            pre_act = pre_act.reshape(cells, hidden)
            gate = 0.5 + 0.5 * jnp.tanh(0.5 * pre_act)
            activated = pre_act * gate
            slope = gate + activated * (1.0 - gate)
            activated = activated.astype(BF16)
            for part in range(2):
                features_of = slice(part * half_hidden, (part + 1) * half_hidden)
                act_buf[part, k, :, lanes] = activated[:, features_of]
                gate_buf[part, k, :, lanes] = slope[:, features_of]
        pred = bias_pair
        for part in range(2):
            pred = pred + lax.dot_general(
                act_buf[part, k],
                weight_pair[part],
                (((1,), (1,)), ((), ())),
                preferred_element_type=F32,
            )
        preds[0, 0, k] = pred.astype(BF16)

    own_copies = []
    sib_copies = []
    act_copies = []
    passed_on = []
    for k in range(CHUNKS):
        forward(k)
        if k == 0:

            @pl.when(own_sum)
            def _():
                pl.semaphore_wait(barrier, members - 1 + members * half_grid - 1)

            @pl.when(jnp.logical_not(own_sum))
            def _():
                pl.semaphore_wait(barrier, members - 1 + members * half_grid)

        across = []
        beyond = []
        for d in range(1, chips):
            to_chip = lax.rem(chip + chips - d, chips)
            copy = member_copy(preds.at[0, 0, k], (d, 0), k, to_chip * 2 + core)
            copy.start()
            across.append(copy)
            if k >= CHUNKS - DIRECT:
                copy = member_copy(preds.at[0, 0, k], (d, 1), k, to_chip * 2 + 1 - core)
                copy.start()
                beyond.append(copy)
        own_copies.append(across)
        passed_on.append(beyond)
        copy = member_copy(preds.at[0, 0, k], (0, 1), k, sibling)
        copy.start()
        sib_copies.append(copy)
        copy = pltpu.make_async_remote_copy(
            src_ref=act_buf.at[1 - core, k],
            dst_ref=sibling_act.at[k],
            send_sem=act_send_sem.at[k],
            recv_sem=act_recv_sem.at[k],
            device_id={"member": sibling},
            device_id_type=mesh_ids,
        )
        copy.start()
        act_copies.append(copy)

    target_load.wait()
    low = lax.broadcasted_iota(jnp.int32, (band_rows, LANES), 1) < channels
    for i in range(half // 2):
        first = target_buf[:, pl.ds(i * LANES, LANES)].astype(F32)
        second = target_buf[:, pl.ds((half // 2 + i) * LANES, LANES)].astype(F32)
        even = jnp.where(low, first, pltpu.roll(second, channels, 1))
        odd = jnp.where(low, pltpu.roll(first, channels, 1), second)
        target_cells[pl.ds(2 * i, band_rows, stride=half), :] = even
        target_cells[pl.ds(2 * i + 1, band_rows, stride=half), :] = odd

    def receive(k):
        for d in range(1, chips):
            own_copies[k][d - 1].wait_recv()
            if k < CHUNKS - DIRECT:
                copy = member_copy(preds.at[d, 0, k], (d, 1), k, sibling)
                copy.start()
                passed_on[k].append(copy)

    pair_scale = 1.0 / (members - 1.0)

    def backward_scores(k):
        own = preds[0, 0, k].astype(F32)
        sib_copies[k].wait_recv()
        sib = preds[0, 1, k].astype(F32)
        observed = target_cells[pl.ds(k * cells, cells), :]
        own_total = smooth_sign(own - sib)
        sib_total = -own_total
        own_score = smooth_sign(own - observed)
        sib_score = smooth_sign(sib - observed)
        for d in range(1, chips):
            passed_on[k][d - 1].wait_recv()
            for other_core in range(2):
                other = preds[d, other_core, k].astype(F32)
                own_total += smooth_sign(own - other)
                sib_total += smooth_sign(sib - other)
        own_grad = own_score - own_total * pair_scale
        sib_grad = sib_score - sib_total * pair_scale
        act_copies[k].wait_recv()
        part = jnp.dot(
            own_grad.T.astype(BF16), act_buf[core, k], preferred_element_type=F32
        ) + jnp.dot(sib_grad.T.astype(BF16), sibling_act[k], preferred_element_type=F32)
        part = part[:channels, :half_hidden] + part[channels:, half_hidden:]
        if k == 0:
            head_acc[...] = part
        else:
            head_acc[...] += part
        return own_grad.astype(BF16)

    def backward_hidden(k, pred_grad):
        for part in range(2):
            act_grad = jnp.dot(pred_grad, weight_pair[part], preferred_element_type=F32)
            grad = (act_grad * gate_buf[part, k]).astype(BF16)
            for side in range(2):
                hidden_grad[
                    0,
                    pl.ds(k * rows, rows),
                    pl.ds(side * half, half),
                    pl.ds(part * half_hidden, half_hidden),
                ] = grad[:, side * half_hidden : (side + 1) * half_hidden].reshape(
                    rows, half, half_hidden
                )

    grads = []
    receive(0)
    for k in range(CHUNKS):
        if k + 1 < CHUNKS:
            receive(k + 1)
        grads.append(backward_scores(k))
        if k < CHUNKS - TAIL:
            backward_hidden(k, grads[k])

    packed = sum_send.shape[1]
    scaled = head_acc[...] * (1.0 / (members * band_rows * columns * grid_count))
    blocks = jnp.concatenate([scaled, scaled], axis=0).T.reshape(half_grid, 2 * packed, LANES)
    lane = lax.broadcasted_iota(jnp.int32, (half_grid, packed, LANES), 2)
    sum_send[...] = jnp.where(
        lane < channels, blocks[:, :packed], blocks[:, packed:]
    ).astype(sum_send.dtype)

    def sum_copy(o, b):
        block = lax.rem(grid + b, half_grid)
        return pltpu.make_async_remote_copy(
            src_ref=sum_send.at[block],
            dst_ref=sum_recv.at[chip, grid],
            send_sem=sum_send_sem.at[o, b],
            recv_sem=sum_recv_sem.at[chip, grid],
            device_id={
                "member": lax.rem(member + o, members),
                "grid": core * half_grid + block,
            },
            device_id_type=mesh_ids,
        )

    for b in reversed(range(half_grid)):
        for o in reversed(range(members)):
            if o == 0 and b == 0:

                @pl.when(jnp.logical_not(own_sum))
                def _():
                    sum_copy(0, 0).start()

                @pl.when(own_sum)
                def _():
                    sum_recv[chip, grid] = sum_send[lax.rem(grid, half_grid)]

            else:
                sum_copy(o, b).start()

    for k in range(CHUNKS - TAIL, CHUNKS):
        backward_hidden(k, grads[k])

    for k in range(CHUNKS):
        sib_copies[k].wait_send()
        act_copies[k].wait_send()
        for copy in own_copies[k]:
            copy.wait_send()
        for copy in passed_on[k]:
            copy.wait_send()

    def arrived(source_chip, source_grid):
        pltpu.make_async_remote_copy(
            src_ref=sum_send.at[0],
            dst_ref=sum_recv.at[source_chip, source_grid],
            send_sem=sum_send_sem.at[0, 0],
            recv_sem=sum_recv_sem.at[source_chip, source_grid],
            device_id={"member": sibling},
            device_id_type=mesh_ids,
        ).wait_recv()

    for q in range(chips):
        for i in range(grid_count):
            wait = functools.partial(
                arrived, lax.rem(chip + q, chips), lax.rem(grid + i, grid_count)
            )
            if q == 0 and i == 0:
                pl.when(jnp.logical_not(own_sum))(wait)
            else:
                wait()
    head = jnp.sum(
        sum_recv[...].astype(F32).reshape(chips * grid_count, packed, LANES), axis=0
    )
    head_grad[...] = jnp.concatenate([head[:, :channels], head[:, channels:]], axis=0)
    for o in range(members):
        for b in range(half_grid):
            if o == 0 and b == 0:

                @pl.when(jnp.logical_not(own_sum))
                def _():
                    sum_copy(0, 0).wait_send()

            else:
                sum_copy(o, b).wait_send()


def local(features, perturbation, target, head_weight, head_bias):
    members = lax.axis_size("member")
    grid_count = lax.axis_size("grid")
    _, band_rows, columns, hidden = features.shape
    channels = head_weight.shape[1]
    half = columns // 2
    rows = band_rows // CHUNKS
    cells = rows * half
    chips = members // 2
    head_rows = hidden // grid_count
    packed = head_rows // 2
    sum_dtype = BF16 if packed % 16 == 0 else F32
    dma = pltpu.SemaphoreType.DMA
    vmem = pl.BlockSpec(memory_space=pltpu.VMEM)
    hbm = pl.BlockSpec(memory_space=pl.ANY)
    return pl.pallas_call(
        functools.partial(kernel, members, grid_count),
        out_shape=(
            pltpu.VMEM(features.shape, BF16),
            jax.ShapeDtypeStruct((head_rows, channels), F32),
        ),
        in_specs=[hbm, hbm, hbm, hbm, hbm],
        out_specs=(vmem, vmem),
        scratch_shapes=[
            pltpu.VMEM((channels, hidden), BF16),
            pltpu.VMEM((1, channels), F32),
            pltpu.VMEM((CHUNKS, rows, columns, hidden), BF16),
            pltpu.VMEM((CHUNKS, rows, columns, hidden), BF16),
            pltpu.VMEM(target.shape, BF16),
            pltpu.VMEM((band_rows * half, LANES), F32),
            pltpu.VMEM((2, 2 * channels, hidden), BF16),
            pltpu.VMEM((2, CHUNKS, cells, hidden), BF16),
            pltpu.VMEM((CHUNKS, cells, hidden), BF16),
            pltpu.VMEM((2, CHUNKS, cells, hidden), F32),
            pltpu.VMEM((chips, 2, CHUNKS, cells, LANES), BF16),
            pltpu.VMEM((channels, hidden // 2), F32),
            pltpu.VMEM((grid_count // 2, packed, LANES), sum_dtype),
            pltpu.VMEM((chips, grid_count, packed, LANES), sum_dtype),
            dma((2, CHUNKS)),
            dma((2,)),
            dma,
            dma((chips, 2, CHUNKS)),
            dma((chips, 2, CHUNKS)),
            dma((CHUNKS,)),
            dma((CHUNKS,)),
            dma((members, grid_count // 2)),
            dma((chips, grid_count)),
        ],
        compiler_params=pltpu.CompilerParams(
            collective_id=0, has_side_effects=True, vmem_limit_bytes=56 * 1024 * 1024
        ),
        cost_estimate=pl.CostEstimate(
            flops=6 * band_rows * columns * hidden * channels,
            bytes_accessed=7 * band_rows * columns * hidden,
            transcendentals=2 * band_rows * columns * hidden,
        ),
    )(features, perturbation, target, head_weight.T, head_bias[None])


def solution(mesh):
    return jax.shard_map(
        local,
        mesh=mesh,
        in_specs=(
            P("member", None, "grid", None),
            P("member", None, "grid", None),
            P(None, "grid"),
            P(),
            P(),
        ),
        out_specs=(P("member", None, "grid", None), P("grid", None)),
        check_vma=False,
    )
```

time: 28.4 us -> 23.6 us (0.83)
  local copies, waits for them, and re-layouts: 6.38 us -> 1.58 us
    unnamed x12 -> x4, local copies, waits for them, and re-layouts: 6.38 us -> 1.58 us
where the time goes in v2:
time: 23.6 us; the launch traced here: 23.5 us
  Pallas kernels  21.2 us (90%)
  local copies, waits for them, and re-layouts  1.58 us (7%)
  between operations  0.65 us (3%)
    pallas_call x1, Pallas kernels, local(): pl.pallas_call(functools.partial(kernel, members, grid_count), out_shape=...  21.2 us
    unnamed x4, local copies, waits for them, and re-layouts  1.58 us

profile of v2, /device:TPU:0, one launch (start us, length us, event | category | flops | bytes accessed | tf_op | source)
XLA Modules:
  0.0 23.5 jit_solution(10130614391620367165)
XLA Ops:
  0.6 21.2 %shard_map.68 = (bf16[1,32,64,256]{3,2,1,0:T(8,128)(2,1)S(1)}, f32[32,64]{1,0:T(8,128)}) custom-call(bf16[1,32,64,256]{3,2,1,0:T(8,128)(2,1)} %features.1, bf16[1,32,64,256]{3,2,1,0:T(8,128)(2,1)} %perturbation.1, bf16[32,4096]{1,0:T(8,128)(2,1)} %target.1, bf16[64,256]{1,0:T(8,128)(2,1)} %bitcast.2, f32[1,64]{1,0:T(1,128)} %bitcast.3), custom_call_target="tpu_custom_call" | custom-call | flops 201326592 | bytes 3670016 | tf_op jit(solution)/shard_map/pallas_call | solution.py:367
  21.9 0.0 copy-start
  21.9 1.0 %copy.9 = bf16[1,32,64,256]{3,2,1,0:T(8,128)(2,1)} copy(bf16[1,32,64,256]{3,2,1,0:T(8,128)(2,1)S(1)} %get-tuple-element.2) | data formatting | bytes 2097152
  22.9 0.0 copy-done
  22.9 0.6 %copy.10 = f32[32,64]{1,0:T(8,128)} copy(f32[32,64]{1,0:T(8,128)S(1)} %copy-done) | data formatting | bytes 16384
Async XLA Ops:
  21.9 1.0 %copy-start = (f32[32,64]{1,0:T(8,128)S(1)}, f32[32,64]{1,0:T(8,128)}, u32[]{:S(2)}) copy-start(f32[32,64]{1,0:T(8,128)} %get-tuple-element.7) | copy-start | bytes 24580

commit v3 on v2

--- a/solution.py
+++ b/solution.py
@@ -10,7 +10,8 @@
 F32 = jnp.float32
 BF16 = jnp.bfloat16
 LANES = 128
-CHUNKS = 8
+EIGHTHS = (1, 2, 2, 2, 1)
+CHUNKS = len(EIGHTHS)
 TAIL = 2
 DIRECT = 1
 
@@ -36,6 +37,7 @@
     target_buf,
     target_cells,
     weight_pair,
+    weight_turned,
     act_buf,
     sibling_act,
     gate_buf,
@@ -58,8 +60,7 @@
     half = columns // 2
     half_hidden = hidden // 2
     half_grid = grid_count // 2
-    rows = band_rows // CHUNKS
-    cells = rows * half
+    starts = [sum(EIGHTHS[:k]) * band_rows // 8 for k in range(CHUNKS + 1)]
     chips = members // 2
     member = lax.axis_index("member")
     grid = lax.axis_index("grid")
@@ -70,6 +71,12 @@
     own_sum = core == owner_core
     mesh_ids = pl.DeviceIdType.MESH
 
+    def row_span(k):
+        return pl.ds(starts[k], starts[k + 1] - starts[k])
+
+    def cell_span(k):
+        return pl.ds(starts[k] * half, (starts[k + 1] - starts[k]) * half)
+
     small_loads = []
     for which, (source, buffer) in enumerate(((weight_hbm, weight_t), (bias_hbm, bias))):
         copy = pltpu.make_async_copy(source, buffer, small_sem.at[which])
@@ -77,15 +84,16 @@
         small_loads.append(copy)
     loads = []
     for k in range(CHUNKS):
-        span = pl.ds(k * rows, rows)
         pair = []
         for which, (source, buffer) in enumerate(((features, feat_buf), (perturbation, pert_buf))):
-            copy = pltpu.make_async_copy(source.at[0, span], buffer.at[k], in_sem.at[which, k])
-            copy.start()
+            copy = pltpu.make_async_copy(
+                source.at[0, row_span(k)], buffer.at[row_span(k)], in_sem.at[which, k]
+            )
             pair.append(copy)
         loads.append(pair)
     target_load = pltpu.make_async_copy(target, target_buf, target_sem)
-    target_load.start()
+    for copy in loads[0]:
+        copy.start()
 
     barrier = pltpu.get_barrier_semaphore()
 
@@ -105,6 +113,10 @@
             else:
                 greet(device)
 
+    for pair in loads[1:]:
+        for copy in pair:
+            copy.start()
+    target_load.start()
     for copy in small_loads:
         copy.wait()
     zero = jnp.zeros((channels, half_hidden), BF16)
@@ -114,12 +126,13 @@
         weight_pair[part, :channels, half_hidden:] = zero
         weight_pair[part, channels:, :half_hidden] = zero
         weight_pair[part, channels:, half_hidden:] = weight_t[:, lanes]
+        weight_turned[part] = weight_pair[part].T
     bias_pair = jnp.concatenate([bias[...], bias[...]], axis=1)
 
     def member_copy(source, slot, k, device):
         return pltpu.make_async_remote_copy(
             src_ref=source,
-            dst_ref=preds.at[slot[0], slot[1], k],
+            dst_ref=preds.at[slot[0], slot[1], cell_span(k)],
             send_sem=pred_send_sem.at[slot[0], slot[1], k],
             recv_sem=pred_recv_sem.at[slot[0], slot[1], k],
             device_id={"member": device},
@@ -132,25 +145,25 @@
         for side in range(2):
             cols = pl.ds(side * half, half)
             lanes = pl.ds(side * half_hidden, half_hidden)
-            pre_act = feat_buf[k, :, cols, :].astype(F32) + pert_buf[k, :, cols, :].astype(F32)
-            pre_act = pre_act.reshape(cells, hidden)
+            pre_act = feat_buf[row_span(k), cols, :].astype(F32) + pert_buf[row_span(k), cols, :].astype(F32)
+            pre_act = pre_act.reshape(-1, hidden)
             gate = 0.5 + 0.5 * jnp.tanh(0.5 * pre_act)
             activated = pre_act * gate
             slope = gate + activated * (1.0 - gate)
             activated = activated.astype(BF16)
             for part in range(2):
                 features_of = slice(part * half_hidden, (part + 1) * half_hidden)
-                act_buf[part, k, :, lanes] = activated[:, features_of]
-                gate_buf[part, k, :, lanes] = slope[:, features_of]
+                act_buf[part, cell_span(k), lanes] = activated[:, features_of]
+                gate_buf[part, cell_span(k), lanes] = slope[:, features_of]
         pred = bias_pair
         for part in range(2):
             pred = pred + lax.dot_general(
-                act_buf[part, k],
-                weight_pair[part],
-                (((1,), (1,)), ((), ())),
+                act_buf[part, cell_span(k), :],
+                weight_turned[part],
+                (((1,), (0,)), ((), ())),
                 preferred_element_type=F32,
             )
-        preds[0, 0, k] = pred.astype(BF16)
+        preds[0, 0, cell_span(k), :] = pred.astype(BF16)
 
     own_copies = []
     sib_copies = []
@@ -172,21 +185,21 @@
         beyond = []
         for d in range(1, chips):
             to_chip = lax.rem(chip + chips - d, chips)
-            copy = member_copy(preds.at[0, 0, k], (d, 0), k, to_chip * 2 + core)
+            copy = member_copy(preds.at[0, 0, cell_span(k)], (d, 0), k, to_chip * 2 + core)
             copy.start()
             across.append(copy)
             if k >= CHUNKS - DIRECT:
-                copy = member_copy(preds.at[0, 0, k], (d, 1), k, to_chip * 2 + 1 - core)
+                copy = member_copy(preds.at[0, 0, cell_span(k)], (d, 1), k, to_chip * 2 + 1 - core)
                 copy.start()
                 beyond.append(copy)
         own_copies.append(across)
         passed_on.append(beyond)
-        copy = member_copy(preds.at[0, 0, k], (0, 1), k, sibling)
+        copy = member_copy(preds.at[0, 0, cell_span(k)], (0, 1), k, sibling)
         copy.start()
         sib_copies.append(copy)
         copy = pltpu.make_async_remote_copy(
-            src_ref=act_buf.at[1 - core, k],
-            dst_ref=sibling_act.at[k],
+            src_ref=act_buf.at[1 - core, cell_span(k)],
+            dst_ref=sibling_act.at[cell_span(k)],
             send_sem=act_send_sem.at[k],
             recv_sem=act_recv_sem.at[k],
             device_id={"member": sibling},
@@ -206,36 +219,38 @@
         target_cells[pl.ds(2 * i + 1, band_rows, stride=half), :] = odd
 
     def receive(k):
-        for d in range(1, chips):
-            own_copies[k][d - 1].wait_recv()
-            if k < CHUNKS - DIRECT:
-                copy = member_copy(preds.at[d, 0, k], (d, 1), k, sibling)
+        if k < CHUNKS - DIRECT:
+            for d in range(1, chips):
+                own_copies[k][d - 1].wait_recv()
+                copy = member_copy(preds.at[d, 0, cell_span(k)], (d, 1), k, sibling)
                 copy.start()
                 passed_on[k].append(copy)
 
     pair_scale = 1.0 / (members - 1.0)
 
     def backward_scores(k):
-        own = preds[0, 0, k].astype(F32)
+        own = preds[0, 0, cell_span(k), :].astype(F32)
         sib_copies[k].wait_recv()
-        sib = preds[0, 1, k].astype(F32)
-        observed = target_cells[pl.ds(k * cells, cells), :]
+        sib = preds[0, 1, cell_span(k), :].astype(F32)
+        observed = target_cells[cell_span(k), :]
         own_total = smooth_sign(own - sib)
         sib_total = -own_total
         own_score = smooth_sign(own - observed)
         sib_score = smooth_sign(sib - observed)
         for d in range(1, chips):
+            if k >= CHUNKS - DIRECT:
+                own_copies[k][d - 1].wait_recv()
             passed_on[k][d - 1].wait_recv()
             for other_core in range(2):
-                other = preds[d, other_core, k].astype(F32)
+                other = preds[d, other_core, cell_span(k), :].astype(F32)
                 own_total += smooth_sign(own - other)
                 sib_total += smooth_sign(sib - other)
         own_grad = own_score - own_total * pair_scale
         sib_grad = sib_score - sib_total * pair_scale
         act_copies[k].wait_recv()
         part = jnp.dot(
-            own_grad.T.astype(BF16), act_buf[core, k], preferred_element_type=F32
-        ) + jnp.dot(sib_grad.T.astype(BF16), sibling_act[k], preferred_element_type=F32)
+            own_grad.T.astype(BF16), act_buf[core, cell_span(k), :], preferred_element_type=F32
+        ) + jnp.dot(sib_grad.T.astype(BF16), sibling_act[cell_span(k), :], preferred_element_type=F32)
         part = part[:channels, :half_hidden] + part[channels:, half_hidden:]
         if k == 0:
             head_acc[...] = part
@@ -246,15 +261,15 @@
     def backward_hidden(k, pred_grad):
         for part in range(2):
             act_grad = jnp.dot(pred_grad, weight_pair[part], preferred_element_type=F32)
-            grad = (act_grad * gate_buf[part, k]).astype(BF16)
+            grad = (act_grad * gate_buf[part, cell_span(k), :]).astype(BF16)
             for side in range(2):
                 hidden_grad[
                     0,
-                    pl.ds(k * rows, rows),
+                    row_span(k),
                     pl.ds(side * half, half),
                     pl.ds(part * half_hidden, half_hidden),
                 ] = grad[:, side * half_hidden : (side + 1) * half_hidden].reshape(
-                    rows, half, half_hidden
+                    -1, half, half_hidden
                 )
 
     grads = []
@@ -288,8 +303,8 @@
             device_id_type=mesh_ids,
         )
 
-    for b in reversed(range(half_grid)):
-        for o in reversed(range(members)):
+    for b in range(half_grid):
+        for o in range(members):
             if o == 0 and b == 0:
 
                 @pl.when(jnp.logical_not(own_sum))
@@ -355,8 +370,7 @@
     _, band_rows, columns, hidden = features.shape
     channels = head_weight.shape[1]
     half = columns // 2
-    rows = band_rows // CHUNKS
-    cells = rows * half
+    cells = band_rows * half
     chips = members // 2
     head_rows = hidden // grid_count
     packed = head_rows // 2
@@ -375,15 +389,16 @@
         scratch_shapes=[
             pltpu.VMEM((channels, hidden), BF16),
             pltpu.VMEM((1, channels), F32),
-            pltpu.VMEM((CHUNKS, rows, columns, hidden), BF16),
-            pltpu.VMEM((CHUNKS, rows, columns, hidden), BF16),
+            pltpu.VMEM((band_rows, columns, hidden), BF16),
+            pltpu.VMEM((band_rows, columns, hidden), BF16),
             pltpu.VMEM(target.shape, BF16),
             pltpu.VMEM((band_rows * half, LANES), F32),
             pltpu.VMEM((2, 2 * channels, hidden), BF16),
-            pltpu.VMEM((2, CHUNKS, cells, hidden), BF16),
-            pltpu.VMEM((CHUNKS, cells, hidden), BF16),
-            pltpu.VMEM((2, CHUNKS, cells, hidden), F32),
-            pltpu.VMEM((chips, 2, CHUNKS, cells, LANES), BF16),
+            pltpu.VMEM((2, hidden, 2 * channels), BF16),
+            pltpu.VMEM((2, cells, hidden), BF16),
+            pltpu.VMEM((cells, hidden), BF16),
+            pltpu.VMEM((2, cells, hidden), F32),
+            pltpu.VMEM((chips, 2, cells, LANES), BF16),
             pltpu.VMEM((channels, hidden // 2), F32),
             pltpu.VMEM((grid_count // 2, packed, LANES), sum_dtype),
             pltpu.VMEM((chips, grid_count, packed, LANES), sum_dtype),

time: 23.6 us -> 23.1 us (0.979)
  Pallas kernels: 21.2 us -> 20.8 us
    pallas_call x1, Pallas kernels: 21.2 us -> 20.8 us  [local(): pl.pallas_call(functools.partial(kernel, members, grid_count), out_shape=...]
where the time goes in v3:
time: 23.1 us; the launch traced here: 23 us
  Pallas kernels  20.8 us (90%)
  local copies, waits for them, and re-layouts  1.58 us (7%)
  between operations  0.65 us (3%)
    pallas_call x1, Pallas kernels, local(): pl.pallas_call(functools.partial(kernel, members, grid_count), out_shape=...  20.8 us
    unnamed x4, local copies, waits for them, and re-layouts  1.58 us

profile of v3, /device:TPU:0, one launch (start us, length us, event | category | flops | bytes accessed | tf_op | source)
XLA Modules:
  0.0 23.0 jit_solution(2759874561881895251)
XLA Ops:
  0.6 20.8 %shard_map.68 = (bf16[1,32,64,256]{3,2,1,0:T(8,128)(2,1)S(1)}, f32[32,64]{1,0:T(8,128)}) custom-call(bf16[1,32,64,256]{3,2,1,0:T(8,128)(2,1)} %features.1, bf16[1,32,64,256]{3,2,1,0:T(8,128)(2,1)} %perturbation.1, bf16[32,4096]{1,0:T(8,128)(2,1)} %target.1, bf16[64,256]{1,0:T(8,128)(2,1)} %bitcast.2, f32[1,64]{1,0:T(1,128)} %bitcast.3), custom_call_target="tpu_custom_call" | custom-call | flops 201326592 | bytes 3670016 | tf_op jit(solution)/shard_map/pallas_call | solution.py:381
  21.4 0.0 copy-start
  21.4 1.0 %copy.9 = bf16[1,32,64,256]{3,2,1,0:T(8,128)(2,1)} copy(bf16[1,32,64,256]{3,2,1,0:T(8,128)(2,1)S(1)} %get-tuple-element.2) | data formatting | bytes 2097152
  22.4 0.0 copy-done
  22.4 0.6 %copy.10 = f32[32,64]{1,0:T(8,128)} copy(f32[32,64]{1,0:T(8,128)S(1)} %copy-done) | data formatting | bytes 16384
Async XLA Ops:
  21.4 1.0 %copy-start = (f32[32,64]{1,0:T(8,128)S(1)}, f32[32,64]{1,0:T(8,128)}, u32[]{:S(2)}) copy-start(f32[32,64]{1,0:T(8,128)} %get-tuple-element.7) | copy-start | bytes 24580

commit v4 on v3

--- a/solution.py
+++ b/solution.py
@@ -382,7 +382,7 @@
         functools.partial(kernel, members, grid_count),
         out_shape=(
             pltpu.VMEM(features.shape, BF16),
-            jax.ShapeDtypeStruct((head_rows, channels), F32),
+            pltpu.VMEM((head_rows, channels), F32),
         ),
         in_specs=[hbm, hbm, hbm, hbm, hbm],
         out_specs=(vmem, vmem),

time: 23.1 us -> 22.5 us (0.974)
  Pallas kernels: 20.8 us -> 20.2 us
    pallas_call x1, Pallas kernels: 20.8 us -> 20.2 us  [local(): pl.pallas_call(functools.partial(kernel, members, grid_count), out_shape=...]
    unnamed x4 -> x2, local copies, waits for them, and re-layouts: 1.58 us -> 1.58 us
where the time goes in v4:
time: 22.5 us; the launch traced here: 22.4 us
  Pallas kernels  20.2 us (90%)
  local copies, waits for them, and re-layouts  1.58 us (7%)
  between operations  0.64 us (3%)
    pallas_call x1, Pallas kernels, local(): pl.pallas_call(functools.partial(kernel, members, grid_count), out_shape=...  20.2 us
    unnamed x2, local copies, waits for them, and re-layouts  1.58 us

profile of v4, /device:TPU:0, one launch (start us, length us, event | category | flops | bytes accessed | tf_op | source)
XLA Modules:
  0.0 22.4 jit_solution(16555400564060706816)
XLA Ops:
  0.6 20.2 %shard_map.68 = (bf16[1,32,64,256]{3,2,1,0:T(8,128)(2,1)S(1)}, f32[32,64]{1,0:T(8,128)S(1)}) custom-call(bf16[1,32,64,256]{3,2,1,0:T(8,128)(2,1)} %features.1, bf16[1,32,64,256]{3,2,1,0:T(8,128)(2,1)} %perturbation.1, bf16[32,4096]{1,0:T(8,128)(2,1)} %target.1, bf16[64,256]{1,0:T(8,128)(2,1)} %bitcast.2, f32[1,64]{1,0:T(1,128)} %bitcast.3), custom_call_target="tpu_custom_call" | custom-call | flops 201326592 | bytes 3670016 | tf_op jit(solution)/shard_map/pallas_call | solution.py:381
  20.8 1.0 %copy.9 = bf16[1,32,64,256]{3,2,1,0:T(8,128)(2,1)} copy(bf16[1,32,64,256]{3,2,1,0:T(8,128)(2,1)S(1)} %get-tuple-element.2) | data formatting | bytes 2097152
  21.8 0.6 %copy.10 = f32[32,64]{1,0:T(8,128)} copy(f32[32,64]{1,0:T(8,128)S(1)} %get-tuple-element.3) | data formatting | bytes 16384
